TPU v7x, 512 devices: a whole 4x8x8 slice. The times are simulated.
512 devices in a mesh: tm: 32 (over y_hi, x, core), feat: 16 (over z, y_lo).
Axes of the slice: x: 4, y: 8 (y_hi: 4, y_lo: 2; y = y_hi * 2 + y_lo), z: 8, core: 2. Of those that a mesh axis runs over, the one named last changes fastest.
Arguments:
- frames: float32 [8192, 8192], P('tm', 'feat'), as said below
Outputs:
- cov_instant: float32 [8192, 8192], P('feat', 'tm')
- cov_lagged: float32 [8192, 8192], P('feat', 'tm')
- cov_later: float32 [8192, 8192], P('feat', 'tm')
Inputs may be any that keep to these rules, and one draw needn't show every extreme that they name: `frames`: real-valued features of a molecular trajectory; entries are of order one to some tens.
All inputs are finite; a program needn't handle non-finite values.
Results may differ from a plain program's by a relative error of at most 0.00051.
Values may be sent and summed in bfloat16 or wider, within the bound.
A program may use at most 64 MiB of HBM per device.

v0:
```python
import jax
import jax.numpy as jnp
from jax import lax
from jax.sharding import PartitionSpec as P

LAG = 256


def broadcast(block, axis, holder):
    block = jnp.where(lax.axis_index(axis) == holder, block, jnp.zeros_like(block))
    return lax.psum(block, axis)


def on_device(frames):
    frame_count, panel_width = frames.shape
    tm_devices = lax.axis_size("tm")
    feat_devices = lax.axis_size("feat")
    total_frames = frame_count * tm_devices
    kept_frames = total_frames - LAG
    block_width = panel_width * feat_devices // tm_devices
    per_panel = tm_devices // feat_devices
    column_sums = lax.psum(jnp.sum(frames, axis=0), "tm")
    centred = (frames - column_sums / total_frames).astype(jnp.bfloat16)
    position = lax.axis_index("tm")
    source_panel = position // per_panel
    column_start = position % per_panel * block_width
    contract = (((0,), (0,)), ((), ()))
    row_panel = lax.all_gather(centred, "tm", axis=0, tiled=True)
    own_block = lax.dynamic_slice_in_dim(row_panel, column_start, block_width, 1)
    col_block = broadcast(own_block, "feat", source_panel)
    head_rows = row_panel[:kept_frames]
    tail_rows = row_panel[LAG:]
    cov_instant = lax.dot_general(
        head_rows, col_block[:kept_frames], contract, preferred_element_type=jnp.float32
    )
    cov_lagged = lax.dot_general(
        head_rows, col_block[LAG:], contract, preferred_element_type=jnp.float32
    )
    cov_later = lax.dot_general(
        tail_rows, col_block[LAG:], contract, preferred_element_type=jnp.float32
    )
    return (cov_instant / kept_frames, cov_lagged / kept_frames, cov_later / kept_frames)


def solution(mesh):
    return jax.shard_map(
        on_device,
        mesh=mesh,
        in_specs=(P("tm", "feat"),),
        out_specs=(P("feat", "tm"), P("feat", "tm"), P("feat", "tm")),
        check_vma=False,
    )
```

profile of v0, /device:TPU:1, one launch (start us, length us, event | category | flops | bytes accessed | tf_op | source)
XLA Modules:
  0.0 402.9 jit_solution(5809584582968191240)
XLA Ops:
  7.2 0.0 all-gather.2.cloned.1.call-start
  7.2 1.1 reduce_sum.9
  8.3 76.1 %psum.14 = f32[512]{0:T(512)S(1)} all-reduce(f32[512]{0:T(512)S(1)} %reduce_sum.9), channel_id=1, replica_groups=mesh['tm'=32,'feat'=16] {'tm'}, use_global_device_ids=true, to_apply=%region_1.0 | all-reduce | flops 512 | bytes 4096 | tf_op jit(solution)/shard_map/psum | solution.py:22
  84.4 1.8 subtract_convert_fusion
  86.2 0.0 all-gather.2.cloned.1.call-update
  86.2 0.0 all-reduce.2.cloned.1.call-start
  86.3 80.7 %all-gather.2.cloned.1.call-done = bf16[8192,512]{1,0:T(8,128)(2,1)} async-done(((bf16[256,512]{1,0:T(8,128)(2,1)}), bf16[8192,512]{1,0:T(8,128)(2,1)}) %all-gather.2.cloned.1.call-update) | async-done | bytes 8388624 | tf_op jit(solution)/shard_map/all_gather | solution.py:28
  167.0 4.9 %dynamic-slice_select_fusion = bf16[8192,256]{1,0:T(8,128)(2,1)} fusion(bf16[8192,512]{1,0:T(8,128)(2,1)} %all-gather.2.cloned.1.call-done, s32[]{:T(128)S(6)} %select_n.25, pred[]{:T(512)S(6)} %eq.5), kind=kLoop, calls=%fused_computation.6 | loop fusion | flops 2097152 | bytes 8388613 | tf_op jit(solution)/shard_map/jit(_where)/select_n | solution.py:10
  171.9 0.0 all-reduce.2.cloned.1.call-update
  171.9 206.9 %all-reduce.2.cloned.1.call-done = bf16[8192,256]{1,0:T(8,128)(2,1)} async-done(((bf16[8192,256]{1,0:T(8,128)(2,1)}), bf16[8192,256]{1,0:T(8,128)(2,1)}) %all-reduce.2.cloned.1.call-update) | async-done | bytes 4194320 | tf_op jit(solution)/shard_map/psum | solution.py:11
  378.7 0.0 copy-start
  378.7 0.0 slice-start
  378.7 7.7 %fusion.19 = f32[512,256]{1,0:T(8,128)} fusion(bf16[8192,256]{1,0:T(8,128)(2,1)} %all-reduce.2.cloned.1.call-done, bf16[8192,512]{1,0:T(8,128)(2,1)} %all-gather.2.cloned.1.call-done), kind=kOutput, calls=%fused_computation.12 | convolution fusion | flops 2080505856 | bytes 12713984 | tf_op jit(solution)/shard_map/dot_general | solution.py:39
  386.5 0.0 copy-done
  386.5 0.0 slice-start.1
  386.5 6.5 %fusion.14 = f32[512,256]{1,0:T(8,128)} fusion(bf16[8192,256]{1,0:T(8,128)(2,1)S(1)} %copy-done, bf16[8192,512]{1,0:T(8,128)(2,1)} %all-gather.2.cloned.1.call-done), kind=kOutput, calls=%fused_computation.11 | convolution fusion | flops 2080505856 | bytes 12713984 | tf_op jit(solution)/shard_map/dot_general | solution.py:36
  393.0 0.0 slice-done
  393.0 0.0 slice-done.1
  393.0 3.1 fusion.9
  (2 shorter events, 0.0 us)
Async XLA Ops:
  7.2 159.8 %all-gather.2.cloned.1.call-start = ((), (), s32[]{:S(2)}) async-start(), calls=%async_computation | async-start | bytes 8650752 | tf_op jit(solution)/shard_map/all_gather | solution.py:28
  86.2 292.5 %all-reduce.2.cloned.1.call-start = ((), (), s32[]{:S(2)}) async-start(), calls=%async_computation.1 | async-start | bytes 8388608 | tf_op jit(solution)/shard_map/psum | solution.py:11
  378.7 7.7 %copy-start = (bf16[8192,256]{1,0:T(8,128)(2,1)S(1)}, bf16[8192,256]{1,0:T(8,128)(2,1)}, u32[]{:S(2)}) copy-start(bf16[8192,256]{1,0:T(8,128)(2,1)} %all-reduce.2.cloned.1.call-done) | copy-start | bytes 12582916
  378.7 14.3 %slice-start = ((s8[8388608]{0:T(1024)(128)(4,1)}), s8[4194304]{0:T(1024)(128)(4,1)S(1)}, s32[]{:S(2)}) async-start(s8[8388608]{0:T(1024)(128)(4,1)} %bitcast), calls=%async_computation.2 | async-start | bytes 8388608
  386.5 6.6 %slice-start.1 = ((s8[8388608]{0:T(1024)(128)(4,1)}), s8[4194304]{0:T(1024)(128)(4,1)S(1)}, s32[]{:S(2)}) async-start(s8[8388608]{0:T(1024)(128)(4,1)} %bitcast), calls=%async_computation.3 | async-start | bytes 8388608
Sparse Core Ops, SparseCore 0:
  86.3 80.5 all-gather.1
  172.0 206.6 all-reduce.1
where the time goes:
time: 403 us
  waiting for transfers between devices  288 us (71%)
  blocking collectives  76.1 us (19%)
  matrix products  17.3 us (4%)
  between operations  14.1 us (3%)
  other arithmetic  7.76 us (2%)
    psum x1, waiting for transfers between devices, broadcast(): return lax.psum(block, axis)  207 us
    all_gather x1, waiting for transfers between devices, on_device(): row_panel = lax.all_gather(centred, 'tm', axis=0, tiled=True)  80.7 us
    psum x1, blocking collectives, on_device(): column_sums = lax.psum(jnp.sum(frames, axis=0), 'tm')  76.1 us
  transfers between devices with their start and end apart: 2, of which 2 were waited for; matrix products, arithmetic and copies ran while one was open for 0% of the time, Pallas kernels for 0%

commit v1 on v0

v1 whole, which is shorter than its diff:
```python
import functools

import jax
import jax.numpy as jnp
from jax import lax
from jax.experimental import pallas as pl
from jax.experimental.pallas import tpu as pltpu
from jax.sharding import PartitionSpec as P

LAG = 256
MESH = pl.DeviceIdType.MESH

NYH, NX, NZ = 4, 4, 8
NT = NYH * NX
N_COPIES = 80


def mod(a, n):
    return lax.rem(a + n, n)


def kernel(
    x_hbm, inst, lagged, later, xv, halves, pair, sums, rows, cols, in_sem, send_sem, recv_sem, turn_sem
):
    tm = lax.axis_index("tm")
    feat = lax.axis_index("feat")
    c = lax.rem(tm, 2)
    t = tm // 2
    yh, x = t // NX, lax.rem(t, NX)
    z, yl = feat // 2, lax.rem(feat, 2)
    p = feat
    diagonal = t == p

    def device(dyh=0, dx=0, dz=0, core=c, yl=yl):
        return {
            "tm": (mod(yh + dyh, NYH) * NX + mod(x + dx, NX)) * 2 + core,
            "feat": mod(z + dz, NZ) * 2 + yl,
        }

    peers = [(a, b) for a in range(NYH) for b in range(NX) if a or b]

    barrier = pltpu.get_barrier_semaphore()
    load = pltpu.make_async_copy(x_hbm, xv, in_sem)
    load.start()
    near = [device(core=1 - c), device(dz=1), device(dz=-1), device(yl=1 - yl)]
    near += [device(dyh=a, dx=b) for a, b in peers]
    for who in near:
        pl.semaphore_signal(barrier, inc=1, device_id=who, device_id_type=MESH)

    @pl.when(jnp.logical_not(diagonal))
    def _():
        for h in range(2):
            pl.semaphore_signal(
                barrier, inc=1, device_id={"tm": 2 * p + h, "feat": t}, device_id_type=MESH
            )

    load.wait()
    column_sums = jnp.sum(xv[...], axis=0, keepdims=True)
    for k in range(4):
        pair[0, k : k + 1, :] = column_sums[:, 128 * k : 128 * (k + 1)]
        pair[0, 4 + k : 5 + k, :] = column_sums[:, 128 * k : 128 * (k + 1)]
    pl.semaphore_wait(barrier, len(near) + 2 * (1 - diagonal.astype(jnp.int32)))

    sent = []

    def send(src, dst, who):
        k = len(sent)
        copy = pltpu.make_async_remote_copy(
            src_ref=src,
            dst_ref=dst,
            send_sem=send_sem.at[k],
            recv_sem=recv_sem.at[k],
            device_id=who,
            device_id_type=MESH,
        )
        copy.start()
        sent.append(copy)
        return copy

    send(pair.at[0], pair.at[1], device(core=1 - c)).wait_recv()
    sums[t] = pair[0] + pair[1]
    arrivals = [send(sums.at[t], sums.at[t], device(dyh=a, dx=b)) for a, b in peers]
    for copy in arrivals:
        copy.wait_recv()
    total = sums[0]
    for k in range(1, NT):
        total = total + sums[k]
    mean = total / (LAG * 2 * NT)

    lanes = pl.ds(pl.multiple_of(c * LAG, LAG), LAG)
    for k in range(4):
        part = (xv[:, 128 * k : 128 * (k + 1)] - mean[k : k + 1, :]).astype(jnp.bfloat16)
        halves[k // 2, :, 128 * (k % 2) : 128 * (k % 2 + 1)] = part
        rows[t, 128 * k : 128 * (k + 1), lanes] = part.T

    def row(dyh, dx, half=None):
        s = mod(yh + dyh, NYH) * NX + mod(x + dx, NX)
        if half is None:
            return rows.at[s, :, lanes]
        return rows.at[s, pl.ds(256 * half, 256), lanes]

    def col(dz, side, half=None):
        s = mod(z + dz, NZ) * 2 + side
        if half is None:
            return cols.at[pl.ds(pl.multiple_of(s * 512, 512), 512), :]
        return cols.at[pl.ds(pl.multiple_of(s * 512 + 256 * half, 256), 256), :]

    def turned(half):
        return cols.at[pl.ds(pl.multiple_of(t * 512 + half * 256, 256), 256), :]

    for h in range(2):
        itself = jnp.logical_and(diagonal, c == h)
        copy = pltpu.make_async_remote_copy(
            src_ref=halves.at[h],
            dst_ref=turned(c),
            send_sem=turn_sem.at[h],
            recv_sem=turn_sem.at[2 + c],
            device_id={"tm": 2 * p + h, "feat": t},
            device_id_type=MESH,
        )
        local = pltpu.make_async_copy(halves.at[h], turned(c), turn_sem.at[2 + c])

        @pl.when(itself)
        def _():
            local.start()

        @pl.when(jnp.logical_not(itself))
        def _():
            copy.start()

    def both(dyh, dx):
        return (
            send(row(dyh, dx), row(dyh, dx), device(dx=1)),
            send(row(dyh, dx), row(dyh, dx), device(dx=-1)),
        )

    def far_x(dyh):
        return (
            send(row(dyh, -1, 0), row(dyh, -1, 0), device(dx=1)),
            send(row(dyh, 1, 1), row(dyh, 1, 1), device(dx=-1)),
        )

    twins = []

    def twin(dyh, dx):
        twins.append(send(row(dyh, dx), row(dyh, dx), device(core=1 - c)))

    def wait(copies):
        for copy in copies:
            copy.wait_recv()

    def z_both(plus, minus, side, halved=False):
        a, b = (0, 1) if halved else (None, None)
        return (
            send(col(plus, side, a), col(plus, side, a), device(dz=1)),
            send(col(minus, side, b), col(minus, side, b), device(dz=-1)),
        )

    y_near = (
        send(row(0, 0), row(0, 0), device(dyh=1)),
        send(row(0, 0), row(0, 0), device(dyh=-1)),
    )
    x_own = both(0, 0)
    twin(0, 0)

    for h in range(2):
        pltpu.make_async_copy(halves.at[h], col(0, yl, h), turn_sem.at[2 + h]).wait()
    own1 = z_both(0, 0, yl)
    cross0 = send(col(0, yl), col(0, yl), device(yl=1 - yl))

    wait(x_own)
    x_own_far = far_x(0)
    twin(0, -1)
    twin(0, 1)

    wait(own1)
    own2 = z_both(-1, 1, yl)
    cross1 = send(col(-1, yl), col(-1, yl), device(yl=1 - yl))
    wait([cross0])
    other1m = send(col(0, 1 - yl), col(0, 1 - yl), device(dz=-1))

    wait(y_near)
    y_far = (
        send(row(-1, 0, 0), row(-1, 0, 0), device(dyh=1)),
        send(row(1, 0, 1), row(1, 0, 1), device(dyh=-1)),
    )
    x_before = both(-1, 0)
    x_after = both(1, 0)
    twin(-1, 0)
    twin(1, 0)
    wait(x_own_far)
    twin(0, 2)

    wait([cross1])
    other1p = send(col(-1, 1 - yl), col(-1, 1 - yl), device(dz=1))
    wait(own2)
    own3 = z_both(-2, 2, yl)

    wait(x_before)
    x_before_far = far_x(-1)
    twin(-1, -1)
    twin(-1, 1)
    wait(y_far)
    x_last = both(2, 0)
    twin(2, 0)

    wait([other1m, other1p])
    other2 = z_both(-2, 1, 1 - yl)

    wait(x_after)
    x_after_far = far_x(1)
    twin(1, -1)
    twin(1, 1)
    wait(own3)
    own4 = z_both(-3, 3, yl, halved=True)
    wait(x_before_far)
    twin(-1, 2)
    wait(other2)
    other3 = z_both(-3, 2, 1 - yl)
    wait(x_last)
    x_last_far = far_x(2)
    twin(2, -1)
    twin(2, 1)
    wait(x_after_far)
    twin(1, 2)
    wait(x_last_far)
    twin(2, 2)
    wait(own4)
    wait(other3)
    wait(twins)

    def product(lhs, rhs):
        return jnp.dot(lhs, rhs, preferred_element_type=jnp.float32)

    kept = LAG * (2 * NT - 1)
    inst[...] = product(rows[0, :, LAG:], cols[LAG : 2 * LAG, :])
    lagged[...] = product(rows[0], cols[LAG : 3 * LAG, :])

    @pl.loop(1, NT - 1)
    def _(s):
        inst[...] += product(rows[s], cols[pl.ds(pl.multiple_of(s * 512, 512), 512), :])
        lagged[...] += product(rows[s], cols[pl.ds(pl.multiple_of(s * 512 + 256, 256), 512), :])

    last = NT - 1
    head = rows[last, :, :LAG]
    middle = inst[...] + product(head, cols[512 * last : 512 * last + LAG, :])
    lagged[...] = (lagged[...] + product(head, cols[512 * last + LAG :, :])) / kept
    inst[...] = (middle + product(rows[0, :, :LAG], cols[:LAG, :])) / kept
    later[...] = (middle + product(rows[last, :, LAG:], cols[512 * last + LAG :, :])) / kept

    for copy in sent:
        copy.wait_send()
    for h in range(2):

        @pl.when(jnp.logical_not(jnp.logical_and(diagonal, c == h)))
        def _():
            pltpu.make_async_copy(halves.at[h], halves.at[h], turn_sem.at[h]).wait()


def on_device(frames):
    frame_count, panel = frames.shape
    block = jax.ShapeDtypeStruct((panel, frame_count), jnp.float32)
    vmem = pl.BlockSpec(memory_space=pltpu.VMEM)
    return pl.pallas_call(
        kernel,
        out_shape=(block, block, block),
        in_specs=[pl.BlockSpec(memory_space=pl.ANY)],
        out_specs=(vmem, vmem, vmem),
        scratch_shapes=[
            pltpu.VMEM((frame_count, panel), jnp.float32),
            pltpu.VMEM((2, frame_count, panel // 2), jnp.bfloat16),
            pltpu.VMEM((2, 8, 128), jnp.float32),
            pltpu.VMEM((NT, 8, 128), jnp.float32),
            pltpu.VMEM((NT, panel, 2 * frame_count), jnp.bfloat16),
            pltpu.VMEM((NT * 2 * frame_count, panel // 2), jnp.bfloat16),
            pltpu.SemaphoreType.DMA,
            pltpu.SemaphoreType.DMA((N_COPIES,)),
            pltpu.SemaphoreType.DMA((N_COPIES,)),
            pltpu.SemaphoreType.DMA((4,)),
        ],
        compiler_params=pltpu.CompilerParams(
            collective_id=0, has_side_effects=True, vmem_limit_bytes=40 * 1024 * 1024
        ),
        cost_estimate=pl.CostEstimate(
            flops=4 * panel * frame_count * 8192, bytes_accessed=1 << 21, transcendentals=0
        ),
    )(frames)


def solution(mesh):
    return jax.shard_map(
        on_device,
        mesh=mesh,
        in_specs=(P("tm", "feat"),),
        out_specs=(P("feat", "tm"), P("feat", "tm"), P("feat", "tm")),
        check_vma=False,
    )
```

time: 403 us -> 134 us (0.33)
  the two profiles are of different devices: /device:TPU:1 before, /device:TPU:200 now
where the time goes in v1:
time: 134 us
  Pallas kernels  130 us (97%)
  local copies, waits for them, and re-layouts  3.42 us (3%)
    pallas_call x1, Pallas kernels, on_device(): pl.pallas_call(kernel, out_shape=(block, block, block), in_specs=[pl.Bloc...  130 us
    unnamed x5, local copies, waits for them, and re-layouts  3.42 us

profile of v1, /device:TPU:200, one launch (start us, length us, event | category | flops | bytes accessed | tf_op | source)
XLA Modules:
  0.0 133.7 jit_solution(4061640879748392287)
XLA Ops:
  0.6 0.0 copy-start
  0.6 1.0 copy-done
  1.7 129.7 %shard_map.38 = (f32[512,256]{1,0:T(8,128)S(1)}, f32[512,256]{1,0:T(8,128)S(1)}, f32[512,256]{1,0:T(8,128)S(1)}) custom-call(f32[256,512]{1,0:T(8,128)S(1)} %copy-done), custom_call_target="tpu_custom_call" | custom-call | flops 4294967296 | bytes 2097152 | tf_op jit(solution)/shard_map/pallas_call | solution.py:264
  131.4 0.8 copy.7
  132.2 0.8 copy.8
  132.9 0.8 copy.9
Async XLA Ops:
  0.6 1.0 copy-start

commit v2 on v1

--- a/solution.py
+++ b/solution.py
@@ -20,7 +20,7 @@
 
 
 def kernel(
-    x_hbm, inst, lagged, later, xv, halves, pair, sums, rows, cols, in_sem, send_sem, recv_sem, turn_sem
+    x_hbm, inst, lagged, later, xv, halves, passing, pair, sums, rows, cols, in_sem, send_sem, recv_sem, turn_sem
 ):
     tm = lax.axis_index("tm")
     feat = lax.axis_index("feat")
@@ -29,7 +29,17 @@
     yh, x = t // NX, lax.rem(t, NX)
     z, yl = feat // 2, lax.rem(feat, 2)
     p = feat
-    diagonal = t == p
+    plane = mod(x // 2 - 2 * yh - z + NZ, NZ)
+    passed = 2 * plane + yl
+
+    def block_at(z, side):
+        shift = t // 2 + z
+        high = lax.rem(shift, 2)
+        return mod(high - shift + 2 * NZ, NZ) // 2 * NX + 2 * high + side
+
+    mine = block_at(z, yl)
+    in_plane = plane == z
+    stays = jnp.logical_and(passed == t, mine == t)
 
     def device(dyh=0, dx=0, dz=0, core=c, yl=yl):
         return {
@@ -47,19 +57,25 @@
     for who in near:
         pl.semaphore_signal(barrier, inc=1, device_id=who, device_id_type=MESH)
 
-    @pl.when(jnp.logical_not(diagonal))
+    @pl.when(jnp.logical_not(stays))
     def _():
         for h in range(2):
             pl.semaphore_signal(
-                barrier, inc=1, device_id={"tm": 2 * p + h, "feat": t}, device_id_type=MESH
+                barrier, inc=1, device_id={"tm": 2 * mine + h, "feat": 2 * z + lax.rem(x, 2)}, device_id_type=MESH
             )
+
+    mirror = {"tm": tm, "feat": 2 * plane + yl}
+
+    @pl.when(jnp.logical_not(in_plane))
+    def _():
+        pl.semaphore_signal(barrier, inc=1, device_id=mirror, device_id_type=MESH)
 
     load.wait()
     column_sums = jnp.sum(xv[...], axis=0, keepdims=True)
     for k in range(4):
         pair[0, k : k + 1, :] = column_sums[:, 128 * k : 128 * (k + 1)]
         pair[0, 4 + k : 5 + k, :] = column_sums[:, 128 * k : 128 * (k + 1)]
-    pl.semaphore_wait(barrier, len(near) + 2 * (1 - diagonal.astype(jnp.int32)))
+    pl.semaphore_wait(barrier, len(near) + 3 - 2 * stays.astype(jnp.int32) - in_plane.astype(jnp.int32))
 
     sent = []
 
@@ -100,7 +116,7 @@
         return rows.at[s, pl.ds(256 * half, 256), lanes]
 
     def col(dz, side, half=None):
-        s = mod(z + dz, NZ) * 2 + side
+        s = block_at(mod(z + dz, NZ), side)
         if half is None:
             return cols.at[pl.ds(pl.multiple_of(s * 512, 512), 512), :]
         return cols.at[pl.ds(pl.multiple_of(s * 512 + 256 * half, 256), 256), :]
@@ -109,16 +125,36 @@
         return cols.at[pl.ds(pl.multiple_of(t * 512 + half * 256, 256), 256), :]
 
     for h in range(2):
-        itself = jnp.logical_and(diagonal, c == h)
         copy = pltpu.make_async_remote_copy(
             src_ref=halves.at[h],
+            dst_ref=passing.at[h],
+            send_sem=turn_sem.at[h],
+            recv_sem=turn_sem.at[2 + h],
+            device_id=mirror,
+            device_id_type=MESH,
+        )
+        local = pltpu.make_async_copy(halves.at[h], passing.at[h], turn_sem.at[2 + h])
+
+        @pl.when(in_plane)
+        def _():
+            local.start()
+
+        @pl.when(jnp.logical_not(in_plane))
+        def _():
+            copy.start()
+
+    def turn(h):
+        itself = jnp.logical_and(stays, c == h)
+        pltpu.make_async_copy(halves.at[h], passing.at[h], turn_sem.at[2 + h]).wait()
+        copy = pltpu.make_async_remote_copy(
+            src_ref=passing.at[h],
             dst_ref=turned(c),
-            send_sem=turn_sem.at[h],
-            recv_sem=turn_sem.at[2 + c],
-            device_id={"tm": 2 * p + h, "feat": t},
+            send_sem=turn_sem.at[4 + h],
+            recv_sem=turn_sem.at[6 + c],
+            device_id={"tm": 2 * passed + h, "feat": 2 * z + lax.rem(x, 2)},
             device_id_type=MESH,
         )
-        local = pltpu.make_async_copy(halves.at[h], turned(c), turn_sem.at[2 + c])
+        local = pltpu.make_async_copy(passing.at[h], turned(c), turn_sem.at[6 + c])
 
         @pl.when(itself)
         def _():
@@ -163,8 +199,10 @@
     x_own = both(0, 0)
     twin(0, 0)
 
+    turn(0)
+    turn(1)
     for h in range(2):
-        pltpu.make_async_copy(halves.at[h], col(0, yl, h), turn_sem.at[2 + h]).wait()
+        pltpu.make_async_copy(passing.at[h], col(0, yl, h), turn_sem.at[6 + h]).wait()
     own1 = z_both(0, 0, yl)
     cross0 = send(col(0, yl), col(0, yl), device(yl=1 - yl))
 
@@ -252,9 +290,13 @@
         copy.wait_send()
     for h in range(2):
 
-        @pl.when(jnp.logical_not(jnp.logical_and(diagonal, c == h)))
+        @pl.when(jnp.logical_not(in_plane))
         def _():
             pltpu.make_async_copy(halves.at[h], halves.at[h], turn_sem.at[h]).wait()
+
+        @pl.when(jnp.logical_not(jnp.logical_and(stays, c == h)))
+        def _():
+            pltpu.make_async_copy(passing.at[h], passing.at[h], turn_sem.at[4 + h]).wait()
 
 
 def on_device(frames):
@@ -269,6 +311,7 @@
         scratch_shapes=[
             pltpu.VMEM((frame_count, panel), jnp.float32),
             pltpu.VMEM((2, frame_count, panel // 2), jnp.bfloat16),
+            pltpu.VMEM((2, frame_count, panel // 2), jnp.bfloat16),
             pltpu.VMEM((2, 8, 128), jnp.float32),
             pltpu.VMEM((NT, 8, 128), jnp.float32),
             pltpu.VMEM((NT, panel, 2 * frame_count), jnp.bfloat16),
@@ -276,7 +319,7 @@
             pltpu.SemaphoreType.DMA,
             pltpu.SemaphoreType.DMA((N_COPIES,)),
             pltpu.SemaphoreType.DMA((N_COPIES,)),
-            pltpu.SemaphoreType.DMA((4,)),
+            pltpu.SemaphoreType.DMA((8,)),
         ],
         compiler_params=pltpu.CompilerParams(
             collective_id=0, has_side_effects=True, vmem_limit_bytes=40 * 1024 * 1024

time: 134 us -> 102 us (0.76)
  the two profiles are of different devices: /device:TPU:200 before, /device:TPU:1 now
where the time goes in v2:
time: 102 us
  Pallas kernels  98 us (96%)
  local copies, waits for them, and re-layouts  3.42 us (3%)
    pallas_call x1, Pallas kernels, on_device(): pl.pallas_call(kernel, out_shape=(block, block, block), in_specs=[pl.Bloc...  98 us
    unnamed x5, local copies, waits for them, and re-layouts  3.42 us

profile of v2, /device:TPU:1, one launch (start us, length us, event | category | flops | bytes accessed | tf_op | source)
XLA Modules:
  0.0 102.1 jit_solution(4091545534192550525)
XLA Ops:
  0.6 0.0 copy-start
  0.6 1.0 %copy-done = f32[256,512]{1,0:T(8,128)S(1)} copy-done((f32[256,512]{1,0:T(8,128)S(1)}, f32[256,512]{1,0:T(8,128)}, u32[]{:S(2)}) %copy-start) | copy-done | bytes 524312
  1.7 98.0 %shard_map.38 = (f32[512,256]{1,0:T(8,128)S(1)}, f32[512,256]{1,0:T(8,128)S(1)}, f32[512,256]{1,0:T(8,128)S(1)}) custom-call(f32[256,512]{1,0:T(8,128)S(1)} %copy-done), custom_call_target="tpu_custom_call" | custom-call | flops 4294967296 | bytes 2097152 | tf_op jit(solution)/shard_map/pallas_call | solution.py:306
  99.7 0.8 copy.7
  100.5 0.8 copy.8
  101.3 0.8 copy.9
Async XLA Ops:
  0.6 1.0 %copy-start = (f32[256,512]{1,0:T(8,128)S(1)}, f32[256,512]{1,0:T(8,128)}, u32[]{:S(2)}) copy-start(f32[256,512]{1,0:T(8,128)} %x_hbm.1) | copy-start | bytes 1572868

commit v3 on v2

--- a/solution.py
+++ b/solution.py
@@ -20,7 +20,7 @@
 
 
 def kernel(
-    x_hbm, inst, lagged, later, xv, halves, passing, pair, sums, rows, cols, in_sem, send_sem, recv_sem, turn_sem
+    x_hbm, inst, lagged, later, xv, halves, passing, means, table, passing_table, other_table, middle, rows, cols, in_sem, send_sem, recv_sem, turn_sem
 ):
     tm = lax.axis_index("tm")
     feat = lax.axis_index("feat")
@@ -71,10 +71,15 @@
         pl.semaphore_signal(barrier, inc=1, device_id=mirror, device_id_type=MESH)
 
     load.wait()
-    column_sums = jnp.sum(xv[...], axis=0, keepdims=True)
+    lanes = pl.ds(pl.multiple_of(c * LAG, LAG), LAG)
+    block_mean = jnp.sum(xv[...], axis=0, keepdims=True) / LAG
     for k in range(4):
-        pair[0, k : k + 1, :] = column_sums[:, 128 * k : 128 * (k + 1)]
-        pair[0, 4 + k : 5 + k, :] = column_sums[:, 128 * k : 128 * (k + 1)]
+        mean = block_mean[:, 128 * k : 128 * (k + 1)]
+        means[c, t, k : k + 1, :] = mean
+        means[c, t, 4 + k : 5 + k, :] = mean
+        part = (xv[:, 128 * k : 128 * (k + 1)] - mean).astype(jnp.bfloat16)
+        halves[k // 2, :, 128 * (k % 2) : 128 * (k % 2 + 1)] = part
+        rows[t, 128 * k : 128 * (k + 1), lanes] = part.T
     pl.semaphore_wait(barrier, len(near) + 3 - 2 * stays.astype(jnp.int32) - in_plane.astype(jnp.int32))
 
     sent = []
@@ -93,22 +98,6 @@
         sent.append(copy)
         return copy
 
-    send(pair.at[0], pair.at[1], device(core=1 - c)).wait_recv()
-    sums[t] = pair[0] + pair[1]
-    arrivals = [send(sums.at[t], sums.at[t], device(dyh=a, dx=b)) for a, b in peers]
-    for copy in arrivals:
-        copy.wait_recv()
-    total = sums[0]
-    for k in range(1, NT):
-        total = total + sums[k]
-    mean = total / (LAG * 2 * NT)
-
-    lanes = pl.ds(pl.multiple_of(c * LAG, LAG), LAG)
-    for k in range(4):
-        part = (xv[:, 128 * k : 128 * (k + 1)] - mean[k : k + 1, :]).astype(jnp.bfloat16)
-        halves[k // 2, :, 128 * (k % 2) : 128 * (k % 2 + 1)] = part
-        rows[t, 128 * k : 128 * (k + 1), lanes] = part.T
-
     def row(dyh, dx, half=None):
         s = mod(yh + dyh, NYH) * NX + mod(x + dx, NX)
         if half is None:
@@ -124,16 +113,16 @@
     def turned(half):
         return cols.at[pl.ds(pl.multiple_of(t * 512 + half * 256, 256), 256), :]
 
-    for h in range(2):
+    def along_z(src, dst, k):
         copy = pltpu.make_async_remote_copy(
-            src_ref=halves.at[h],
-            dst_ref=passing.at[h],
-            send_sem=turn_sem.at[h],
-            recv_sem=turn_sem.at[2 + h],
+            src_ref=src,
+            dst_ref=dst,
+            send_sem=turn_sem.at[k],
+            recv_sem=turn_sem.at[2 + k],
             device_id=mirror,
             device_id_type=MESH,
         )
-        local = pltpu.make_async_copy(halves.at[h], passing.at[h], turn_sem.at[2 + h])
+        local = pltpu.make_async_copy(src, dst, turn_sem.at[2 + k])
 
         @pl.when(in_plane)
         def _():
@@ -143,18 +132,17 @@
         def _():
             copy.start()
 
-    def turn(h):
+    def within_plane(src, dst, h, send_k, recv_k):
         itself = jnp.logical_and(stays, c == h)
-        pltpu.make_async_copy(halves.at[h], passing.at[h], turn_sem.at[2 + h]).wait()
         copy = pltpu.make_async_remote_copy(
-            src_ref=passing.at[h],
-            dst_ref=turned(c),
-            send_sem=turn_sem.at[4 + h],
-            recv_sem=turn_sem.at[6 + c],
+            src_ref=src,
+            dst_ref=dst,
+            send_sem=turn_sem.at[send_k],
+            recv_sem=turn_sem.at[recv_k],
             device_id={"tm": 2 * passed + h, "feat": 2 * z + lax.rem(x, 2)},
             device_id_type=MESH,
         )
-        local = pltpu.make_async_copy(passing.at[h], turned(c), turn_sem.at[6 + c])
+        local = pltpu.make_async_copy(src, dst, turn_sem.at[recv_k])
 
         @pl.when(itself)
         def _():
@@ -163,6 +151,16 @@
         @pl.when(jnp.logical_not(itself))
         def _():
             copy.start()
+
+    def landed(ref, k):
+        pltpu.make_async_copy(ref, ref, turn_sem.at[k]).wait()
+
+    for h in range(2):
+        along_z(halves.at[h], passing.at[h], h)
+
+    def turn(h):
+        landed(passing.at[h], 2 + h)
+        within_plane(passing.at[h], turned(c), h, 4 + h, 6 + c)
 
     def both(dyh, dx):
         return (
@@ -191,6 +189,9 @@
             send(col(plus, side, a), col(plus, side, a), device(dz=1)),
             send(col(minus, side, b), col(minus, side, b), device(dz=-1)),
         )
+
+    def cross(dz):
+        return send(col(dz, yl), col(dz, yl), device(yl=1 - yl))
 
     y_near = (
         send(row(0, 0), row(0, 0), device(dyh=1)),
@@ -201,10 +202,11 @@
 
     turn(0)
     turn(1)
+    mean_arrivals = [send(means.at[c, t], means.at[c, t], device(dyh=a, dx=b)) for a, b in peers]
     for h in range(2):
-        pltpu.make_async_copy(passing.at[h], col(0, yl, h), turn_sem.at[6 + h]).wait()
+        landed(passing.at[h], 6 + h)
     own1 = z_both(0, 0, yl)
-    cross0 = send(col(0, yl), col(0, yl), device(yl=1 - yl))
+    cross0 = cross(0)
 
     wait(x_own)
     x_own_far = far_x(0)
@@ -213,9 +215,7 @@
 
     wait(own1)
     own2 = z_both(-1, 1, yl)
-    cross1 = send(col(-1, yl), col(-1, yl), device(yl=1 - yl))
-    wait([cross0])
-    other1m = send(col(0, 1 - yl), col(0, 1 - yl), device(dz=-1))
+    cross1 = (cross(-1), cross(1))
 
     wait(y_near)
     y_far = (
@@ -229,32 +229,46 @@
     wait(x_own_far)
     twin(0, 2)
 
-    wait([cross1])
-    other1p = send(col(-1, 1 - yl), col(-1, 1 - yl), device(dz=1))
+    wait(mean_arrivals)
+    mean_twin = send(means.at[c], means.at[c], device(core=1 - c))
+
     wait(own2)
     own3 = z_both(-2, 2, yl)
+    wait([mean_twin])
+    for s in range(NT):
+        for core in range(2):
+            for k in range(4):
+                line = 2 * s + core
+                table[k // 2, line : line + 1, 128 * (k % 2) : 128 * (k % 2 + 1)] = means[core, s, k : k + 1, :]
+
+    along_z(table.at[c], passing_table, 8)
 
     wait(x_before)
     x_before_far = far_x(-1)
     twin(-1, -1)
     twin(-1, 1)
+    wait([cross0])
+    wait(cross1)
+    other1 = z_both(-1, 1, 1 - yl)
     wait(y_far)
     x_last = both(2, 0)
     twin(2, 0)
 
-    wait([other1m, other1p])
-    other2 = z_both(-2, 1, 1 - yl)
+    wait(own3)
+    own4 = z_both(-3, 3, yl, halved=True)
 
     wait(x_after)
     x_after_far = far_x(1)
     twin(1, -1)
     twin(1, 1)
-    wait(own3)
-    own4 = z_both(-3, 3, yl, halved=True)
     wait(x_before_far)
     twin(-1, 2)
-    wait(other2)
-    other3 = z_both(-3, 2, 1 - yl)
+    landed(passing_table, 10)
+    within_plane(passing_table, other_table, c, 9, 11)
+    wait(other1)
+    other2 = z_both(-2, 2, 1 - yl)
+    wait(own4)
+    cross4 = cross(4)
     wait(x_last)
     x_last_far = far_x(2)
     twin(2, -1)
@@ -263,47 +277,83 @@
     twin(1, 2)
     wait(x_last_far)
     twin(2, 2)
-    wait(own4)
-    wait(other3)
+    wait([cross4])
+    wait(other2)
     wait(twins)
 
     def product(lhs, rhs):
         return jnp.dot(lhs, rhs, preferred_element_type=jnp.float32)
 
-    kept = LAG * (2 * NT - 1)
-    inst[...] = product(rows[0, :, LAG:], cols[LAG : 2 * LAG, :])
-    lagged[...] = product(rows[0], cols[LAG : 3 * LAG, :])
+    def split(value):
+        high = value.astype(jnp.bfloat16).astype(jnp.float32)
+        return high, value - high
+
+    landed(other_table, 11)
+    high, low = split(other_table[...] - jnp.sum(other_table[...], axis=0, keepdims=True) / (2 * NT))
+    nothing = jnp.zeros((1, LAG), jnp.float32)
+
+    def three(value):
+        return jnp.concatenate(
+            [
+                jnp.concatenate([value[:-1], nothing], axis=0),
+                jnp.concatenate([value[1:], nothing], axis=0),
+                jnp.concatenate([nothing, value[1:]], axis=0),
+            ],
+            axis=1,
+        ).astype(jnp.bfloat16)
+
+    high, low = three(high), three(low)
+    right = jnp.concatenate([high, low, high], axis=0)
+    for h in range(2):
+        mine_high, mine_low = split(table[h] - jnp.sum(table[h], axis=0, keepdims=True) / (2 * NT))
+        left = jnp.concatenate([mine_high, mine_high, mine_low], axis=0).T.astype(jnp.bfloat16)
+        between = product(left, right) * LAG
+        part = pl.ds(256 * h, 256)
+        inst[part, :] = between[:, :LAG]
+        lagged[part, :] = between[:, LAG : 2 * LAG]
+        later[part, :] = between[:, 2 * LAG :]
+
+    last = NT - 1
+    head = rows[last, :, :LAG]
+    middle[...] = product(rows[0, :, LAG:], cols[LAG : 2 * LAG, :]) + product(
+        head, cols[512 * last : 512 * last + LAG, :]
+    )
+    lagged[...] += product(rows[0], cols[LAG : 3 * LAG, :])
 
     @pl.loop(1, NT - 1)
     def _(s):
-        inst[...] += product(rows[s], cols[pl.ds(pl.multiple_of(s * 512, 512), 512), :])
+        middle[...] += product(rows[s], cols[pl.ds(pl.multiple_of(s * 512, 512), 512), :])
         lagged[...] += product(rows[s], cols[pl.ds(pl.multiple_of(s * 512 + 256, 256), 512), :])
 
-    last = NT - 1
-    head = rows[last, :, :LAG]
-    middle = inst[...] + product(head, cols[512 * last : 512 * last + LAG, :])
-    lagged[...] = (lagged[...] + product(head, cols[512 * last + LAG :, :])) / kept
-    inst[...] = (middle + product(rows[0, :, :LAG], cols[:LAG, :])) / kept
-    later[...] = (middle + product(rows[last, :, LAG:], cols[512 * last + LAG :, :])) / kept
+    lagged[...] += product(head, cols[512 * last + LAG :, :])
+    inst[...] += middle[...] + product(rows[0, :, :LAG], cols[:LAG, :])
+    later[...] += middle[...] + product(rows[last, :, LAG:], cols[512 * last + LAG :, :])
 
     for copy in sent:
         copy.wait_send()
+
+    @pl.when(jnp.logical_not(in_plane))
+    def _():
+        for h in range(2):
+            landed(halves.at[h], h)
+        landed(passing_table, 8)
+
     for h in range(2):
 
-        @pl.when(jnp.logical_not(in_plane))
-        def _():
-            pltpu.make_async_copy(halves.at[h], halves.at[h], turn_sem.at[h]).wait()
-
         @pl.when(jnp.logical_not(jnp.logical_and(stays, c == h)))
         def _():
-            pltpu.make_async_copy(passing.at[h], passing.at[h], turn_sem.at[4 + h]).wait()
+            landed(passing.at[h], 4 + h)
+
+    @pl.when(jnp.logical_not(stays))
+    def _():
+        landed(passing_table, 9)
 
 
 def on_device(frames):
     frame_count, panel = frames.shape
     block = jax.ShapeDtypeStruct((panel, frame_count), jnp.float32)
     vmem = pl.BlockSpec(memory_space=pltpu.VMEM)
-    return pl.pallas_call(
+    sums = pl.pallas_call(
         kernel,
         out_shape=(block, block, block),
         in_specs=[pl.BlockSpec(memory_space=pl.ANY)],
@@ -312,14 +362,17 @@
             pltpu.VMEM((frame_count, panel), jnp.float32),
             pltpu.VMEM((2, frame_count, panel // 2), jnp.bfloat16),
             pltpu.VMEM((2, frame_count, panel // 2), jnp.bfloat16),
-            pltpu.VMEM((2, 8, 128), jnp.float32),
-            pltpu.VMEM((NT, 8, 128), jnp.float32),
+            pltpu.VMEM((2, NT, 8, 128), jnp.float32),
+            pltpu.VMEM((2, 2 * NT, LAG), jnp.float32),
+            pltpu.VMEM((2 * NT, LAG), jnp.float32),
+            pltpu.VMEM((2 * NT, LAG), jnp.float32),
+            pltpu.VMEM((panel, frame_count), jnp.float32),
             pltpu.VMEM((NT, panel, 2 * frame_count), jnp.bfloat16),
             pltpu.VMEM((NT * 2 * frame_count, panel // 2), jnp.bfloat16),
             pltpu.SemaphoreType.DMA,
             pltpu.SemaphoreType.DMA((N_COPIES,)),
             pltpu.SemaphoreType.DMA((N_COPIES,)),
-            pltpu.SemaphoreType.DMA((8,)),
+            pltpu.SemaphoreType.DMA((12,)),
         ],
         compiler_params=pltpu.CompilerParams(
             collective_id=0, has_side_effects=True, vmem_limit_bytes=40 * 1024 * 1024
@@ -328,6 +381,8 @@
             flops=4 * panel * frame_count * 8192, bytes_accessed=1 << 21, transcendentals=0
         ),
     )(frames)
+    kept = LAG * (2 * NT - 1)
+    return tuple(value / kept for value in sums)
 
 
 def solution(mesh):

time: 102 us -> 94.2 us (0.924)
  Pallas kernels: 98 us -> 90.5 us
  local copies, waits for them, and re-layouts: 3.42 us -> 1.03 us
  other arithmetic: 0 us -> 1.9 us
    pallas_call x1, Pallas kernels: 98 us -> 90.5 us  [on_device(): pl.pallas_call(kernel, out_shape=(block, block, block), in_specs=[pl.Bloc...]
    unnamed x5 -> x2, local copies, waits for them, and re-layouts: 3.42 us -> 1.03 us
    div x0 -> x2, other arithmetic: none -> 1.9 us  [on_device(): return tuple((value / kept for value in sums))]
where the time goes in v3:
time: 94.2 us; the launch traced here: 94 us
  Pallas kernels  90.5 us (96%)
  other arithmetic  1.9 us (2%)
  local copies, waits for them, and re-layouts  1.03 us (1%)
    pallas_call x1, Pallas kernels, on_device(): pl.pallas_call(kernel, out_shape=(block, block, block), in_specs=[pl.Bloc...  90.5 us
    div x2, other arithmetic, on_device(): return tuple((value / kept for value in sums))  1.9 us

profile of v3, /device:TPU:1, one launch (start us, length us, event | category | flops | bytes accessed | tf_op | source)
XLA Modules:
  0.0 94.0 jit_solution(11370500345178722354)
XLA Ops:
  0.6 0.0 copy-start
  0.6 1.0 %copy-done = f32[256,512]{1,0:T(8,128)S(1)} copy-done((f32[256,512]{1,0:T(8,128)S(1)}, f32[256,512]{1,0:T(8,128)}, u32[]{:S(2)}) %copy-start) | copy-done | bytes 524312
  1.7 90.5 %shard_map.38 = (f32[512,256]{1,0:T(8,128)S(1)}, f32[512,256]{1,0:T(8,128)S(1)}, f32[512,256]{1,0:T(8,128)S(1)}) custom-call(f32[256,512]{1,0:T(8,128)S(1)} %copy-done), custom_call_target="tpu_custom_call" | custom-call | flops 4294967296 | bytes 2097152 | tf_op jit(solution)/shard_map/pallas_call | solution.py:356
  92.1 0.8 broadcast_multiply_fusion.2
  93.0 1.1 %broadcast_multiply_fusion = (f32[512,256]{1,0:T(8,128)}, f32[512,256]{1,0:T(8,128)}) fusion(f32[512,256]{1,0:T(8,128)S(1)} %get-tuple-element.8, f32[512,256]{1,0:T(8,128)S(1)} %get-tuple-element.7), kind=kLoop, calls=%fused_computation | loop fusion | flops 262144 | bytes 2097152 | tf_op jit(solution)/shard_map/div | solution.py:385
Async XLA Ops:
  0.6 1.0 %copy-start = (f32[256,512]{1,0:T(8,128)S(1)}, f32[256,512]{1,0:T(8,128)}, u32[]{:S(2)}) copy-start(f32[256,512]{1,0:T(8,128)} %x_hbm.1) | copy-start | bytes 1572868

commit v4 on v3

--- a/solution.py
+++ b/solution.py
@@ -12,7 +12,7 @@
 
 NYH, NX, NZ = 4, 4, 8
 NT = NYH * NX
-N_COPIES = 80
+N_COPIES = 100
 
 
 def mod(a, n):
@@ -29,17 +29,28 @@
     yh, x = t // NX, lax.rem(t, NX)
     z, yl = feat // 2, lax.rem(feat, 2)
     p = feat
-    plane = mod(x // 2 - 2 * yh - z + NZ, NZ)
-    passed = 2 * plane + yl
+    def placed(yh, x, z, yl):
+        odd = lax.rem(x, 2)
+        steps = lax.rem(2 * lax.rem(x // 2 + x, 2) + lax.rem(yh // 2 + yh, 2) + 2 * yl, 4)
+        return lax.rem((5 - 2 * odd) * z + 2 * steps + odd, NZ), lax.rem(yh, 2)
+
+    odd = lax.rem(x, 2)
+    factor = 5 - 2 * odd
+    offset = lax.rem(placed(yh, x, 0, yl)[0], NZ)
+    plane, side_to = placed(yh, x, z, yl)
+    origin = lax.rem(factor * (z - offset + 2 * NZ), NZ)
+    passed = 2 * origin + yl
 
     def block_at(z, side):
-        shift = t // 2 + z
-        high = lax.rem(shift, 2)
-        return mod(high - shift + 2 * NZ, NZ) // 2 * NX + 2 * high + side
+        z_from = t // 2
+        low = lax.rem(z + z_from, 2)
+        steps = lax.rem(z - (5 - 2 * low) * z_from - low + 8 * NZ, NZ) // 2
+        steps = lax.rem(steps + 2 * lax.rem(t, 2), 4)
+        return (2 * lax.rem(steps + side, 2) + side) * NX + 2 * lax.rem(steps // 2 + low, 2) + low
 
     mine = block_at(z, yl)
     in_plane = plane == z
-    stays = jnp.logical_and(passed == t, mine == t)
+    stays = jnp.logical_and(passed == t, side_to == yl)
 
     def device(dyh=0, dx=0, dz=0, core=c, yl=yl):
         return {
@@ -61,14 +72,16 @@
     def _():
         for h in range(2):
             pl.semaphore_signal(
-                barrier, inc=1, device_id={"tm": 2 * mine + h, "feat": 2 * z + lax.rem(x, 2)}, device_id_type=MESH
+                barrier, inc=1, device_id={"tm": 2 * mine + h, "feat": 2 * z + lax.rem(t, 2)}, device_id_type=MESH
             )
 
-    mirror = {"tm": tm, "feat": 2 * plane + yl}
+    ahead = {"tm": tm, "feat": 2 * plane + yl}
 
     @pl.when(jnp.logical_not(in_plane))
     def _():
-        pl.semaphore_signal(barrier, inc=1, device_id=mirror, device_id_type=MESH)
+        pl.semaphore_signal(
+            barrier, inc=1, device_id={"tm": tm, "feat": passed}, device_id_type=MESH
+        )
 
     load.wait()
     lanes = pl.ds(pl.multiple_of(c * LAG, LAG), LAG)
@@ -119,7 +132,7 @@
             dst_ref=dst,
             send_sem=turn_sem.at[k],
             recv_sem=turn_sem.at[2 + k],
-            device_id=mirror,
+            device_id=ahead,
             device_id_type=MESH,
         )
         local = pltpu.make_async_copy(src, dst, turn_sem.at[2 + k])
@@ -139,7 +152,7 @@
             dst_ref=dst,
             send_sem=turn_sem.at[send_k],
             recv_sem=turn_sem.at[recv_k],
-            device_id={"tm": 2 * passed + h, "feat": 2 * z + lax.rem(x, 2)},
+            device_id={"tm": 2 * passed + h, "feat": 2 * z + side_to},
             device_id_type=MESH,
         )
         local = pltpu.make_async_copy(src, dst, turn_sem.at[recv_k])
@@ -155,6 +168,7 @@
     def landed(ref, k):
         pltpu.make_async_copy(ref, ref, turn_sem.at[k]).wait()
 
+    mean_arrivals = [send(means.at[c, t], means.at[c, t], device(dyh=a, dx=b)) for a, b in peers]
     for h in range(2):
         along_z(halves.at[h], passing.at[h], h)
 
@@ -183,15 +197,14 @@
         for copy in copies:
             copy.wait_recv()
 
-    def z_both(plus, minus, side, halved=False):
-        a, b = (0, 1) if halved else (None, None)
+    def z_both(plus, minus, side, part):
         return (
-            send(col(plus, side, a), col(plus, side, a), device(dz=1)),
-            send(col(minus, side, b), col(minus, side, b), device(dz=-1)),
-        )
-
-    def cross(dz):
-        return send(col(dz, yl), col(dz, yl), device(yl=1 - yl))
+            send(col(plus, side, part), col(plus, side, part), device(dz=1)),
+            send(col(minus, side, part), col(minus, side, part), device(dz=-1)),
+        )
+
+    def cross(dz, part):
+        return send(col(dz, yl, part), col(dz, yl, part), device(yl=1 - yl))
 
     y_near = (
         send(row(0, 0), row(0, 0), device(dyh=1)),
@@ -200,86 +213,104 @@
     x_own = both(0, 0)
     twin(0, 0)
 
-    turn(0)
-    turn(1)
-    mean_arrivals = [send(means.at[c, t], means.at[c, t], device(dyh=a, dx=b)) for a, b in peers]
-    for h in range(2):
-        landed(passing.at[h], 6 + h)
-    own1 = z_both(0, 0, yl)
-    cross0 = cross(0)
-
     wait(x_own)
     x_own_far = far_x(0)
     twin(0, -1)
     twin(0, 1)
-
-    wait(own1)
-    own2 = z_both(-1, 1, yl)
-    cross1 = (cross(-1), cross(1))
-
+    wait(mean_arrivals)
+    mean_twin = send(means.at[c], means.at[c], device(core=1 - c))
+    wait([mean_twin])
+    for s in range(NT):
+        for core in range(2):
+            for k in range(4):
+                line = 2 * s + core
+                table[k // 2, line : line + 1, 128 * (k % 2) : 128 * (k % 2 + 1)] = means[core, s, k : k + 1, :]
+
+    along_z(table.at[c], passing_table, 8)
+    turn(0)
+    turn(1)
     wait(y_near)
     y_far = (
         send(row(-1, 0, 0), row(-1, 0, 0), device(dyh=1)),
         send(row(1, 0, 1), row(1, 0, 1), device(dyh=-1)),
     )
     x_before = both(-1, 0)
-    x_after = both(1, 0)
     twin(-1, 0)
     twin(1, 0)
+    x_after = both(1, 0)
+    own1 = []
+    for part in range(2):
+        landed(passing.at[part], 6 + part)
+        own1.append(z_both(0, 0, yl, part))
+    cross0 = [cross(0, 0), cross(0, 1)]
+    landed(passing_table, 10)
+    within_plane(passing_table, other_table, c, 9, 11)
+
     wait(x_own_far)
     twin(0, 2)
-
-    wait(mean_arrivals)
-    mean_twin = send(means.at[c], means.at[c], device(core=1 - c))
-
-    wait(own2)
-    own3 = z_both(-2, 2, yl)
-    wait([mean_twin])
-    for s in range(NT):
-        for core in range(2):
-            for k in range(4):
-                line = 2 * s + core
-                table[k // 2, line : line + 1, 128 * (k % 2) : 128 * (k % 2 + 1)] = means[core, s, k : k + 1, :]
-
-    along_z(table.at[c], passing_table, 8)
 
     wait(x_before)
     x_before_far = far_x(-1)
     twin(-1, -1)
     twin(-1, 1)
-    wait([cross0])
-    wait(cross1)
-    other1 = z_both(-1, 1, 1 - yl)
+
+    own2, cross1 = [], []
+    for part in range(2):
+        wait(own1[part])
+        own2.append(z_both(-1, 1, yl, part))
+    for part in range(2):
+        cross1.append((cross(-1, part), cross(1, part)))
+
     wait(y_far)
     x_last = both(2, 0)
     twin(2, 0)
-
-    wait(own3)
-    own4 = z_both(-3, 3, yl, halved=True)
 
     wait(x_after)
     x_after_far = far_x(1)
     twin(1, -1)
     twin(1, 1)
-    wait(x_before_far)
-    twin(-1, 2)
-    landed(passing_table, 10)
-    within_plane(passing_table, other_table, c, 9, 11)
-    wait(other1)
-    other2 = z_both(-2, 2, 1 - yl)
-    wait(own4)
-    cross4 = cross(4)
+
+    own3 = []
+    for part in range(2):
+        wait(own2[part])
+        own3.append(z_both(-2, 2, yl, part))
+
+    wait(cross0)
+    other1 = []
+    for part in range(2):
+        wait(cross1[part])
+        other1.append(z_both(-1, 1, 1 - yl, part))
+
     wait(x_last)
     x_last_far = far_x(2)
     twin(2, -1)
     twin(2, 1)
+
+    wait(x_before_far)
+    twin(-1, 2)
+
+    wait(own3[0])
+    wait(own3[1])
+    own4 = (
+        send(col(-3, yl, 0), col(-3, yl, 0), device(dz=1)),
+        send(col(3, yl, 1), col(3, yl, 1), device(dz=-1)),
+    )
+
     wait(x_after_far)
     twin(1, 2)
+
+    other2 = []
+    for part in range(2):
+        wait(other1[part])
+        other2.append(z_both(-2, 2, 1 - yl, part))
+
+    cross4 = []
+    for part in range(2):
+        wait([own4[part]])
+        cross4.append(cross(4, part))
+
     wait(x_last_far)
     twin(2, 2)
-    wait([cross4])
-    wait(other2)
-    wait(twins)
 
     def product(lhs, rhs):
         return jnp.dot(lhs, rhs, preferred_element_type=jnp.float32)
@@ -313,18 +344,40 @@
         lagged[part, :] = between[:, LAG : 2 * LAG]
         later[part, :] = between[:, 2 * LAG :]
 
+    def col_here(s):
+        where, side = placed(s // NX, lax.rem(s, NX), t // 2, lax.rem(t, 2))
+        steps = mod(where - z, NZ)
+        return jnp.logical_or(side == yl, jnp.logical_or(steps < 3, steps > 5))
+
+    def multiply(first):
+        @pl.loop(1, NT - 1)
+        def _(s):
+            both_here = col_here(s)
+            next_here = jnp.logical_and(both_here, col_here(s + 1))
+
+            @pl.when(both_here if first else jnp.logical_not(both_here))
+            def _():
+                middle[...] += product(rows[s], cols[pl.ds(pl.multiple_of(s * 512, 512), 512), :])
+
+            @pl.when(next_here if first else jnp.logical_not(next_here))
+            def _():
+                lagged[...] += product(rows[s], cols[pl.ds(pl.multiple_of(s * 512 + 256, 256), 512), :])
+
+    wait(twins)
+    middle[...] = jnp.zeros_like(middle)
+    multiply(True)
+
+    wait(cross4)
+    for part in range(2):
+        wait(other2[part])
+    multiply(False)
+
     last = NT - 1
     head = rows[last, :, :LAG]
-    middle[...] = product(rows[0, :, LAG:], cols[LAG : 2 * LAG, :]) + product(
+    middle[...] += product(rows[0, :, LAG:], cols[LAG : 2 * LAG, :]) + product(
         head, cols[512 * last : 512 * last + LAG, :]
     )
     lagged[...] += product(rows[0], cols[LAG : 3 * LAG, :])
-
-    @pl.loop(1, NT - 1)
-    def _(s):
-        middle[...] += product(rows[s], cols[pl.ds(pl.multiple_of(s * 512, 512), 512), :])
-        lagged[...] += product(rows[s], cols[pl.ds(pl.multiple_of(s * 512 + 256, 256), 512), :])
-
     lagged[...] += product(head, cols[512 * last + LAG :, :])
     inst[...] += middle[...] + product(rows[0, :, :LAG], cols[:LAG, :])
     later[...] += middle[...] + product(rows[last, :, LAG:], cols[512 * last + LAG :, :])

time: 94.2 us -> 88.9 us (0.944)
  Pallas kernels: 90.5 us -> 85.2 us
    pallas_call x1, Pallas kernels: 90.5 us -> 85.2 us  [on_device(): pl.pallas_call(kernel, out_shape=(block, block, block), in_specs=[pl.Bloc...]
where the time goes in v4:
time: 88.9 us; the launch traced here: 88.8 us
  Pallas kernels  85.2 us (96%)
  other arithmetic  1.9 us (2%)
  local copies, waits for them, and re-layouts  1.03 us (1%)
    pallas_call x1, Pallas kernels, on_device(): pl.pallas_call(kernel, out_shape=(block, block, block), in_specs=[pl.Bloc...  85.2 us
    div x2, other arithmetic, on_device(): return tuple((value / kept for value in sums))  1.9 us

profile of v4, /device:TPU:1, one launch (start us, length us, event | category | flops | bytes accessed | tf_op | source)
XLA Modules:
  0.0 88.8 jit_solution(14994611976830114745)
XLA Ops:
  0.6 0.0 copy-start
  0.6 1.0 %copy-done = f32[256,512]{1,0:T(8,128)S(1)} copy-done((f32[256,512]{1,0:T(8,128)S(1)}, f32[256,512]{1,0:T(8,128)}, u32[]{:S(2)}) %copy-start) | copy-done | bytes 524312
  1.7 85.2 %shard_map.38 = (f32[512,256]{1,0:T(8,128)S(1)}, f32[512,256]{1,0:T(8,128)S(1)}, f32[512,256]{1,0:T(8,128)S(1)}) custom-call(f32[256,512]{1,0:T(8,128)S(1)} %copy-done), custom_call_target="tpu_custom_call" | custom-call | flops 4294967296 | bytes 2097152 | tf_op jit(solution)/shard_map/pallas_call | solution.py:409
  86.9 0.8 broadcast_multiply_fusion.2
  87.7 1.1 %broadcast_multiply_fusion = (f32[512,256]{1,0:T(8,128)}, f32[512,256]{1,0:T(8,128)}) fusion(f32[512,256]{1,0:T(8,128)S(1)} %get-tuple-element.8, f32[512,256]{1,0:T(8,128)S(1)} %get-tuple-element.7), kind=kLoop, calls=%fused_computation | loop fusion | flops 262144 | bytes 2097152 | tf_op jit(solution)/shard_map/div | solution.py:438
Async XLA Ops:
  0.6 1.0 %copy-start = (f32[256,512]{1,0:T(8,128)S(1)}, f32[256,512]{1,0:T(8,128)}, u32[]{:S(2)}) copy-start(f32[256,512]{1,0:T(8,128)} %x_hbm.1) | copy-start | bytes 1572868

commit v5 on v4

--- a/solution.py
+++ b/solution.py
@@ -206,11 +206,11 @@
     def cross(dz, part):
         return send(col(dz, yl, part), col(dz, yl, part), device(yl=1 - yl))
 
+    x_own = both(0, 0)
     y_near = (
         send(row(0, 0), row(0, 0), device(dyh=1)),
         send(row(0, 0), row(0, 0), device(dyh=-1)),
     )
-    x_own = both(0, 0)
     twin(0, 0)
 
     wait(x_own)

time: 88.9 us -> 88.9 us (level)
  no operation moved by 1% of the time
where the time goes in v5:
time: 88.9 us; the launch traced here: 88.8 us
  Pallas kernels  85.2 us (96%)
  other arithmetic  1.9 us (2%)
  local copies, waits for them, and re-layouts  1.03 us (1%)
    pallas_call x1, Pallas kernels, on_device(): pl.pallas_call(kernel, out_shape=(block, block, block), in_specs=[pl.Bloc...  85.2 us
    div x2, other arithmetic, on_device(): return tuple((value / kept for value in sums))  1.9 us

profile of v5, /device:TPU:1, one launch (start us, length us, event | category | flops | bytes accessed | tf_op | source)
XLA Modules:
  0.0 88.8 jit_solution(9474640449756189197)
XLA Ops:
  0.6 0.0 copy-start
  0.6 1.0 %copy-done = f32[256,512]{1,0:T(8,128)S(1)} copy-done((f32[256,512]{1,0:T(8,128)S(1)}, f32[256,512]{1,0:T(8,128)}, u32[]{:S(2)}) %copy-start) | copy-done | bytes 524312
  1.7 85.2 %shard_map.38 = (f32[512,256]{1,0:T(8,128)S(1)}, f32[512,256]{1,0:T(8,128)S(1)}, f32[512,256]{1,0:T(8,128)S(1)}) custom-call(f32[256,512]{1,0:T(8,128)S(1)} %copy-done), custom_call_target="tpu_custom_call" | custom-call | flops 4294967296 | bytes 2097152 | tf_op jit(solution)/shard_map/pallas_call | solution.py:409
  86.9 0.8 broadcast_multiply_fusion.2
  87.7 1.1 %broadcast_multiply_fusion = (f32[512,256]{1,0:T(8,128)}, f32[512,256]{1,0:T(8,128)}) fusion(f32[512,256]{1,0:T(8,128)S(1)} %get-tuple-element.8, f32[512,256]{1,0:T(8,128)S(1)} %get-tuple-element.7), kind=kLoop, calls=%fused_computation | loop fusion | flops 262144 | bytes 2097152 | tf_op jit(solution)/shard_map/div | solution.py:438
Async XLA Ops:
  0.6 1.0 %copy-start = (f32[256,512]{1,0:T(8,128)S(1)}, f32[256,512]{1,0:T(8,128)}, u32[]{:S(2)}) copy-start(f32[256,512]{1,0:T(8,128)} %x_hbm.1) | copy-start | bytes 1572868
